TPU v7x, 32 devices: a whole 2x2x4 slice. The times are simulated.
32 devices in a mesh: groups: 2 (over x), frame: 16 (over z, y, core).
Axes of the slice: x: 2, y: 2, z: 4, core: 2. Of those that a mesh axis runs over, the one named last changes fastest.
Arguments:
- queries: bfloat16 [4096, 2048], P(('groups', 'frame')), parts along dimension 0, may hold values from -40 to 40, as said below
- key_rows: bfloat16 [4096, 2048], P(('groups', 'frame')), parts along dimension 0, may hold values from -4 to 4
- value_rows: bfloat16 [4096, 2048], P(('groups', 'frame')), parts along dimension 0, may hold values from -6 to 6
- slopes: bfloat16 [16], replicated, may hold values from 0.0019989014 to 0.19921875
- noise_level: int32 [32], P('groups'), parts along dimension 0, may hold values from 0 to 999
- frame_times: int32 [32], P('groups'), parts along dimension 0, may hold values from 0 to 30, as said below
Outputs:
- advanced: bfloat16 [4096, 2048], P(('groups', 'frame')), parts along dimension 0
There are 2 independent parts, one for each index of `groups`. A program takes and returns all parts, laid end to end along the dimension named above; an argument that names none is the same for every part. Nothing has to cross between parts.
Inputs may be any that keep to these rules, and one draw needn't show every extreme that they name: Rows of queries may be large multiples of key rows. `frame_times`: strictly increasing along the window, starting at 0; neighbouring frames differ by 1 to 3; the last frame stands at 30.
All inputs are finite; a program needn't handle non-finite values.
Results may differ from a plain program's by a relative error of at most 0.009.
Values may be sent and summed in bfloat16 or wider, within the bound.
A program may use at most 64 MiB of HBM per device.

v0:
```python
import math

import jax
import jax.numpy as jnp
from jax import lax
from jax.sharding import PartitionSpec as P

LEVELS = 1000


def shifted(value, axis, steps):
    count = lax.axis_size(axis)
    first, last = (max(0, -steps), min(count, count - steps))
    return lax.ppermute(value, axis, [(source, source + steps) for source in range(first, last)])


def noise_gates(noise_level):
    phase = (noise_level.astype(jnp.float32) / LEVELS + 0.008) / 1.008
    cosine = jnp.cos(phase * (math.pi / 2))
    signal = cosine * cosine
    return (jnp.sqrt(signal), jnp.sqrt(1.0 - signal))


def spatial_branch(queries, key_rows, value_rows, head_count, head_dim):
    frame_rows = queries.shape[0]
    query_heads = queries.reshape(frame_rows, head_count, head_dim)
    key_heads = key_rows.reshape(frame_rows, head_count, head_dim)
    value_heads = value_rows.reshape(frame_rows, head_count, head_dim)
    scores = jnp.einsum(
        "qhd,khd->hqk", query_heads, key_heads, preferred_element_type=jnp.float32
    ) / math.sqrt(head_dim)
    weights = jax.nn.softmax(scores, axis=-1).astype(jnp.bfloat16)
    attended = jnp.einsum("hqk,khd->qhd", weights, value_heads, preferred_element_type=jnp.float32)
    return attended.reshape(frame_rows, head_count * head_dim)


def temporal_core(query_moved, key_moved, value_moved, slope_vals, distance, noise_gate, head_dim):
    scores = jnp.einsum(
        "qnhd,knhd->nhqk", query_moved, key_moved, preferred_element_type=jnp.float32
    ) / math.sqrt(head_dim)
    penalty = -slope_vals[:, None, None] * distance[None]
    scores = scores + penalty[None]
    weights = jax.nn.softmax(scores, axis=-1).astype(jnp.bfloat16)
    attended = jnp.einsum(
        "nhqk,knhd->qnhd", weights, value_moved, preferred_element_type=jnp.float32
    )
    return (attended * noise_gate[:, None, None, None]).astype(jnp.bfloat16)


def body(queries, key_rows, value_rows, slopes, noise_level, frame_times):
    frame_rows, model_width = queries.shape
    head_count = slopes.shape[0]
    head_dim = model_width // head_count
    signal_gate, noise_gate = noise_gates(noise_level)
    distance = jnp.abs(frame_times[:, None] - frame_times[None, :]).astype(jnp.float32)
    own_gate = lax.dynamic_index_in_dim(signal_gate, lax.axis_index("frame"), 0, keepdims=False)
    query_block = queries.reshape(1, frame_rows, head_count, head_dim)
    key_block = key_rows.reshape(1, frame_rows, head_count, head_dim)
    value_block = value_rows.reshape(1, frame_rows, head_count, head_dim)
    moved_query, moved_key, moved_value = (
        lax.all_to_all(query_block, "frame", split_axis=1, concat_axis=0, tiled=True),
        lax.all_to_all(key_block, "frame", split_axis=1, concat_axis=0, tiled=True),
        lax.all_to_all(value_block, "frame", split_axis=1, concat_axis=0, tiled=True),
    )
    temporal = temporal_core(
        moved_query,
        moved_key,
        moved_value,
        slopes.astype(jnp.float32),
        distance,
        noise_gate,
        head_dim,
    )
    returned = lax.all_to_all(
        jnp.concatenate([temporal[1:], jnp.zeros_like(temporal[:1])], axis=0),
        "frame",
        split_axis=0,
        concat_axis=1,
        tiled=True,
    )
    temporal_rows = returned.reshape(frame_rows, model_width).astype(jnp.float32)
    spatial = spatial_branch(queries, key_rows, value_rows, head_count, head_dim)
    carried = shifted((own_gate * spatial).astype(jnp.bfloat16), "frame", -1).astype(jnp.float32)
    advanced = (carried + temporal_rows).astype(jnp.bfloat16)
    return advanced


def solution(mesh):
    return jax.shard_map(
        body,
        mesh=mesh,
        in_specs=(
            P(("groups", "frame"), None),
            P(("groups", "frame"), None),
            P(("groups", "frame"), None),
            P(),
            P("groups"),
            P("groups"),
        ),
        out_specs=P(("groups", "frame"), None),
        check_vma=False,
    )
```

profile of v0, /device:TPU:13, one launch (start us, length us, event | category | flops | bytes accessed | tf_op | source)
XLA Modules:
  0.0 88.1 jit_solution(10010185706619340784)
XLA Ops:
  0.0 1.9 %copy.39 = bf16[16,8,16,128]{3,2,1,0:T(8,128)(2,1)} copy(bf16[16,8,16,128]{3,1,2,0:T(8,128)(2,1)} %bitcast.63) | data formatting | bytes 1048576
  1.9 6.7 %all-to-all-start = ((bf16[1,128,16,128]{3,2,0,1:T(8,128)(2,1)}), bf16[1,128,16,128]{3,2,0,1:T(8,128)(2,1)S(1)}, u32[]{:S(2)}, u32[]{:S(2)}) async-start(bf16[1,128,16,128]{3,2,0,1:T(8,128)(2,1)} %bitcast.16), calls=%async_computation | async-start | bytes 1048576 | tf_op jit(solution)/shard_map/all_to_all | solution.py:61
  8.6 0.9 %copy.40 = bf16[16,8,16,128]{3,2,1,0:T(8,128)(2,1)} copy(bf16[16,8,16,128]{3,1,2,0:T(8,128)(2,1)S(1)} %bitcast.62) | data formatting | bytes 1048576
  9.5 12.7 %all-to-all-done = bf16[1,128,16,128]{3,2,0,1:T(8,128)(2,1)S(1)} async-done(((bf16[1,128,16,128]{3,2,0,1:T(8,128)(2,1)}), bf16[1,128,16,128]{3,2,0,1:T(8,128)(2,1)S(1)}, u32[]{:S(2)}, u32[]{:S(2)}) %all-to-all-start) | async-done | bytes 524320 | tf_op jit(solution)/shard_map/all_to_all | solution.py:61
  22.2 5.1 %all-to-all-start.1 = ((bf16[1,128,16,128]{3,2,0,1:T(8,128)(2,1)}), bf16[1,128,16,128]{3,2,0,1:T(8,128)(2,1)S(1)}, u32[]{:S(2)}, u32[]{:S(2)}) async-start(bf16[1,128,16,128]{3,2,0,1:T(8,128)(2,1)} %bitcast.20), calls=%async_computation.1 | async-start | bytes 1048576 | tf_op jit(solution)/shard_map/all_to_all | solution.py:62
  27.3 0.0 copy-done
  27.3 0.9 %copy.41 = bf16[16,8,16,128]{3,2,1,0:T(8,128)(2,1)} copy(bf16[16,8,16,128]{3,1,2,0:T(8,128)(2,1)S(1)} %bitcast.61) | data formatting | bytes 1048576
  28.3 12.7 %all-to-all-done.1 = bf16[1,128,16,128]{3,2,0,1:T(8,128)(2,1)S(1)} async-done(((bf16[1,128,16,128]{3,2,0,1:T(8,128)(2,1)}), bf16[1,128,16,128]{3,2,0,1:T(8,128)(2,1)S(1)}, u32[]{:S(2)}, u32[]{:S(2)}) %all-to-all-start.1) | async-done | bytes 524320 | tf_op jit(solution)/shard_map/all_to_all | solution.py:62
  40.9 5.1 %all-to-all-start.2 = ((bf16[1,128,16,128]{3,2,0,1:T(8,128)(2,1)}), bf16[1,128,16,128]{3,2,0,1:T(8,128)(2,1)S(1)}, u32[]{:S(2)}, u32[]{:S(2)}) async-start(bf16[1,128,16,128]{3,2,0,1:T(8,128)(2,1)} %bitcast.24), calls=%async_computation.2 | async-start | bytes 1048576 | tf_op jit(solution)/shard_map/all_to_all | solution.py:63
  46.1 0.1 fusion.26
  46.1 0.3 copy.35
  46.4 0.0 copy-start.5
  46.4 0.7 dynamic_slice.4
  47.1 0.6 copy-done.3
  47.7 0.1 abs_convert_fusion
  47.8 0.1 broadcast_multiply_fusion
  47.9 2.0 %fusion.27 = (f32[8,16,16]{2,1,0:T(8,128)S(1)}, f32[8,16,16,16]{2,3,1,0:T(8,128)}) fusion(bf16[16,8,16,128]{3,2,1,0:T(8,128)(2,1)S(1)} %bitcast.66, bf16[16,8,16,128]{3,2,1,0:T(8,128)(2,1)S(1)} %bitcast.64, f32[16,16,16]{1,2,0:T(8,128)S(1)} %broadcast_multiply_fusion), kind=kOutput, calls=%fused_computation.36 | convolution fusion | flops 8519695 | bytes 1204224 | tf_op jit(solution)/shard_map/sub | solution.py:43
  49.9 9.7 %all-to-all-done.2 = bf16[1,128,16,128]{3,2,0,1:T(8,128)(2,1)S(1)} async-done(((bf16[1,128,16,128]{3,2,0,1:T(8,128)(2,1)}), bf16[1,128,16,128]{3,2,0,1:T(8,128)(2,1)S(1)}, u32[]{:S(2)}, u32[]{:S(2)}) %all-to-all-start.2) | async-done | bytes 524320 | tf_op jit(solution)/shard_map/all_to_all | solution.py:63
  59.6 1.7 %fusion.9 = bf16[16,8,16,128]{3,0,2,1:T(8,128)(2,1)S(1)} fusion(f32[8,16,16,16]{2,3,1,0:T(8,128)} %get-tuple-element.8, bf16[16,8,16,128]{3,2,1,0:T(8,128)(2,1)S(1)} %bitcast.67, f32[16]{0:T(128)S(1)} %get-tuple-element.6, f32[8,16,16]{2,1,0:T(8,128)S(1)} %get-tuple-element.7), kind=kOutput, calls=%fused_computation.13 | convolution fusion | flops 8978432 | bytes 1187904 | tf_op jit(solution)/shard_map/nhqk,knhd->qnhd/dot_general | solution.py:44
  61.4 0.2 slice.4
  61.6 0.1 copy.36
  61.7 0.9 concatenate.3.clone
  62.6 5.1 %all-to-all-start.3 = ((bf16[16,8,16,128]{3,2,1,0:T(8,128)(2,1)}), bf16[16,8,16,128]{3,2,1,0:T(8,128)(2,1)S(1)}, u32[]{:S(2)}, u32[]{:S(2)}) async-start(bf16[16,8,16,128]{3,2,1,0:T(8,128)(2,1)} %concatenate.3.clone), calls=%async_computation.3 | async-start | bytes 1048576 | tf_op jit(solution)/shard_map/all_to_all | solution.py:74
  67.7 0.6 fusion.28
  68.3 0.5 convolution_multiply_fusion.3
  68.8 1.1 %fusion.8 = bf16[16,128,128]{1,2,0:T(8,128)(2,1)S(1)} fusion(bf16[128,16,128]{0,2,1:T(8,128)(2,1)S(1)} %bitcast.65, f32[16,128]{1,0:T(8,128)S(1)} %fusion.28, f32[]{:T(128)} %bitcast, f32[16,128,128]{1,2,0:T(8,128)S(1)} %convolution_multiply_fusion.3), kind=kOutput, calls=%fused_computation.12 | convolution fusion | flops 68421760 | bytes 2105348 | tf_op jit(solution)/shard_map/hqk,khd->qhd/dot_general | solution.py:33
  69.8 0.2 copy.27
  70.0 2.3 %collective-permute-start = (bf16[128,2048]{1,0:T(8,128)(2,1)S(1)}, bf16[128,2048]{1,0:T(8,128)(2,1)S(1)}, u32[]{:S(2)}, u32[]{:S(2)}) collective-permute-start(bf16[128,2048]{1,0:T(8,128)(2,1)S(1)} %copy.27), channel_id=1, source_target_pairs={{1,0},{2,1},{3,2},{4,3},{5,4},{6,5},{7,6},{8,7},{9,8},{10,9},{11,1... | collective-permute-start | bytes 1572872 | tf_op jit(solution)/shard_map/ppermute | solution.py:14
  72.3 9.0 %all-to-all-done.3 = bf16[16,8,16,128]{3,2,1,0:T(8,128)(2,1)S(1)} async-done(((bf16[16,8,16,128]{3,2,1,0:T(8,128)(2,1)}), bf16[16,8,16,128]{3,2,1,0:T(8,128)(2,1)S(1)}, u32[]{:S(2)}, u32[]{:S(2)}) %all-to-all-start.3) | async-done | bytes 524320 | tf_op jit(solution)/shard_map/all_to_all | solution.py:74
  81.3 0.1 convert_bitcast_fusion
  81.4 5.5 %collective-permute-done = bf16[128,2048]{1,0:T(8,128)(2,1)S(1)} collective-permute-done((bf16[128,2048]{1,0:T(8,128)(2,1)S(1)}, bf16[128,2048]{1,0:T(8,128)(2,1)S(1)}, u32[]{:S(2)}, u32[]{:S(2)}) %collective-permute-start) | collective-permute-done | bytes 524320 | tf_op jit(solution)/shard_map/ppermute | solution.py:14
  86.9 1.1 %fusion.10 = bf16[128,2048]{1,0:T(8,128)(2,1)} fusion(f32[16,8,16,128]{3,2,1,0:T(8,128)S(1)} %convert_bitcast_fusion, bf16[128,2048]{1,0:T(8,128)(2,1)S(1)} %collective-permute-done), kind=kLoop, calls=%fused_computation.15 | loop fusion | flops 786432 | bytes 2097152 | tf_op jit(solution)/shard_map/convert_element_type | solution.py:84
  (10 shorter events, 0.0 us)
Async XLA Ops:
  1.9 6.7 %copy-start.1 = (bf16[128,2048]{1,0:T(8,128)(2,1)S(1)}, bf16[128,2048]{1,0:T(8,128)(2,1)}, u32[]{:S(2)}) copy-start(bf16[128,2048]{1,0:T(8,128)(2,1)} %param.7) | copy-start | bytes 1572868
  1.9 20.3 %all-to-all-start = ((bf16[1,128,16,128]{3,2,0,1:T(8,128)(2,1)}), bf16[1,128,16,128]{3,2,0,1:T(8,128)(2,1)S(1)}, u32[]{:S(2)}, u32[]{:S(2)}) async-start(bf16[1,128,16,128]{3,2,0,1:T(8,128)(2,1)} %bitcast.16), calls=%async_computation | async-start | bytes 1048576 | tf_op jit(solution)/shard_map/all_to_all | solution.py:61
  22.2 5.1 %copy-start = (bf16[128,2048]{1,0:T(8,128)(2,1)S(1)}, bf16[128,2048]{1,0:T(8,128)(2,1)}, u32[]{:S(2)}) copy-start(bf16[128,2048]{1,0:T(8,128)(2,1)} %param.8) | copy-start | bytes 1572868
  22.2 18.7 %all-to-all-start.1 = ((bf16[1,128,16,128]{3,2,0,1:T(8,128)(2,1)}), bf16[1,128,16,128]{3,2,0,1:T(8,128)(2,1)S(1)}, u32[]{:S(2)}, u32[]{:S(2)}) async-start(bf16[1,128,16,128]{3,2,0,1:T(8,128)(2,1)} %bitcast.20), calls=%async_computation.1 | async-start | bytes 1048576 | tf_op jit(solution)/shard_map/all_to_all | solution.py:62
  40.9 5.1 %copy-start.4 = (s32[16]{0:T(128)S(1)}, s32[16]{0:T(128)}, u32[]{:S(2)}) copy-start(s32[16]{0:T(128)} %param.10) | copy-start | bytes 196
  40.9 18.7 %all-to-all-start.2 = ((bf16[1,128,16,128]{3,2,0,1:T(8,128)(2,1)}), bf16[1,128,16,128]{3,2,0,1:T(8,128)(2,1)S(1)}, u32[]{:S(2)}, u32[]{:S(2)}) async-start(bf16[1,128,16,128]{3,2,0,1:T(8,128)(2,1)} %bitcast.24), calls=%async_computation.2 | async-start | bytes 1048576 | tf_op jit(solution)/shard_map/all_to_all | solution.py:63
  46.4 0.7 copy-start.5
  47.1 0.7 copy-start.3
  62.6 5.1 %copy-start.2 = (bf16[128,2048]{1,0:T(8,128)(2,1)S(1)}, bf16[128,2048]{1,0:T(8,128)(2,1)}, u32[]{:S(2)}) copy-start(bf16[128,2048]{1,0:T(8,128)(2,1)} %param.6) | copy-start | bytes 1572868
  62.6 18.7 %all-to-all-start.3 = ((bf16[16,8,16,128]{3,2,1,0:T(8,128)(2,1)}), bf16[16,8,16,128]{3,2,1,0:T(8,128)(2,1)S(1)}, u32[]{:S(2)}, u32[]{:S(2)}) async-start(bf16[16,8,16,128]{3,2,1,0:T(8,128)(2,1)} %concatenate.3.clone), calls=%async_computation.3 | async-start | bytes 1048576 | tf_op jit(solution)/shard_map/all_to_all | solution.py:74
  70.0 16.9 %collective-permute-start = (bf16[128,2048]{1,0:T(8,128)(2,1)S(1)}, bf16[128,2048]{1,0:T(8,128)(2,1)S(1)}, u32[]{:S(2)}, u32[]{:S(2)}) collective-permute-start(bf16[128,2048]{1,0:T(8,128)(2,1)S(1)} %copy.27), channel_id=1, source_target_pairs={{1,0},{2,1},{3,2},{4,3},{5,4},{6,5},{7,6},{8,7},{9,8},{10,9},{11,1... | collective-permute-start | bytes 1572872 | tf_op jit(solution)/shard_map/ppermute | solution.py:14
where the time goes:
time: 88.7 us; the launch traced here: 88.1 us
  waiting for transfers between devices  49.6 us (56%)
  starting transfers between devices  24.3 us (27%)
  local copies, waits for them, and re-layouts  6.76 us (8%)
  matrix products  5.85 us (7%)
  other arithmetic  1.45 us (2%)
    all_to_all x1, waiting for transfers between devices, body(): lax.all_to_all(query_block, 'frame', split_axis=1, concat_axis=0, tiled=T...  12.7 us
    all_to_all x1, waiting for transfers between devices, body(): lax.all_to_all(key_block, 'frame', split_axis=1, concat_axis=0, tiled=True)  12.7 us
    all_to_all x1, waiting for transfers between devices, body(): lax.all_to_all(value_block, 'frame', split_axis=1, concat_axis=0, tiled=T...  9.74 us
    all_to_all x1, waiting for transfers between devices, body(): lax.all_to_all(jnp.concatenate([temporal[1:], jnp.zeros_like(temporal[:1]...  8.98 us
    all_to_all x1, starting transfers between devices, body(): lax.all_to_all(query_block, 'frame', split_axis=1, concat_axis=0, tiled=T...  6.69 us
    ppermute x1, waiting for transfers between devices, shifted(): lax.ppermute(value, axis, [(source, source + steps) for source in range(f...  5.51 us
    all_to_all x1, starting transfers between devices, body(): lax.all_to_all(key_block, 'frame', split_axis=1, concat_axis=0, tiled=True)  5.11 us
    all_to_all x1, starting transfers between devices, body(): lax.all_to_all(value_block, 'frame', split_axis=1, concat_axis=0, tiled=T...  5.11 us
  transfers between devices with their start and end apart: 5, of which 5 were waited for; matrix products, arithmetic and copies ran while one was open for 8% of the time, Pallas kernels for 0%

commit v1 on v0

v1 whole, which is shorter than its diff:
```python
import functools
import math

import jax
import jax.numpy as jnp
from jax import lax
from jax.experimental import pallas as pl
from jax.experimental.pallas import tpu as pltpu
from jax.sharding import PartitionSpec as P

LEVELS = 1000
ROWS = 16
LANES = 128
FAR = 1e30
MESH = pl.DeviceIdType.MESH


def softmax_rows(scores):
    top = jnp.max(scores, axis=-1, keepdims=True)
    raised = jnp.exp(scores - top)
    return (raised * (1.0 / jnp.sum(raised, axis=-1, keepdims=True))).astype(jnp.bfloat16)


def scores_of(queries, keys):
    return lax.dot_general(
        queries, keys, (((1,), (1,)), ((), ())), preferred_element_type=jnp.float32
    )


def kernel(
    n, plan,
    slopes_ref, level_ref, times_ref, q_ref, k_ref, v_ref, out_ref,
    qkv, recv, temporal, ret, sent, carried, dist, signal_gate, noise_gate,
    load_sem, send_sem, recv_sem, back_send_sem, back_recv_sem, carry_send_sem, carry_recv_sem,
):
    frame_rows, width, head_count, head_dim, row_blocks, col_blocks, chunks = plan
    block_cols = width // col_blocks
    cols = block_cols // chunks
    total = n * ROWS
    scale = 1.0 / math.sqrt(head_dim)
    me = lax.axis_index("frame")

    loads = [
        pltpu.make_async_copy(source, qkv.at[i], load_sem.at[i])
        for i, source in enumerate((q_ref, k_ref, v_ref))
    ]
    for load in loads:
        load.start()
    barrier = pltpu.get_barrier_semaphore()

    @pl.loop(1, n)
    def _(step):
        pl.semaphore_signal(
            barrier, inc=1, device_id={"frame": lax.rem(me + step, n)}, device_id_type=MESH
        )

    pl.semaphore_wait(barrier, n - 1)
    for load in loads:
        load.wait()

    def piece(peer, chunk):
        row = pl.multiple_of(lax.div(peer, col_blocks) * ROWS, ROWS)
        col = pl.multiple_of(lax.rem(peer, col_blocks) * block_cols + chunk * cols, LANES)
        return qkv.at[:, pl.ds(row, ROWS), pl.ds(col, cols)]

    my_slot = pl.ds(pl.multiple_of(me * ROWS, ROWS), ROWS)
    my_rows = pl.ds(pl.multiple_of(lax.div(me, col_blocks) * ROWS, ROWS), ROWS)
    my_col = pl.ds(pl.multiple_of(lax.rem(me, col_blocks) * cols, LANES), cols)
    first_head = lax.rem(me, col_blocks) * (block_cols // head_dim)

    @pl.loop(0, chunks)
    def _(chunk):
        @pl.loop(1, n)
        def _(step):
            peer = lax.rem(me + step, n)
            pltpu.make_async_remote_copy(
                src_ref=piece(peer, chunk),
                dst_ref=recv.at[chunk, :, my_slot, :],
                send_sem=send_sem.at[chunk],
                recv_sem=recv_sem.at[chunk],
                device_id={"frame": peer},
                device_id_type=MESH,
            ).start()

        pltpu.make_async_copy(
            piece(me, chunk), recv.at[chunk, :, my_slot, :], recv_sem.at[chunk]
        ).start()

    row_frame = lax.broadcasted_iota(jnp.int32, (n, LANES), 0)

    def place(f, level):
        return jnp.where(row_frame == f, level_ref[f].astype(jnp.float32), level)

    level = lax.fori_loop(0, n, place, jnp.zeros((n, LANES), jnp.float32))
    phase = (level / LEVELS + 0.008) / 1.008
    cosine = jnp.cos(phase * (math.pi / 2))
    signal = cosine * cosine
    signal_gate[...] = jnp.sqrt(signal)
    noise_gate[...] = jnp.sqrt(1.0 - signal)

    own_gate = signal_gate[pl.ds(me, 1), :]

    @pl.loop(0, head_count, unroll=4)
    def _(h):
        at = pl.ds(pl.multiple_of(h * head_dim, LANES), head_dim)
        weights = softmax_rows(scores_of(qkv[0, :, at], qkv[1, :, at]) * scale)
        attended = jnp.dot(weights, qkv[2, :, at], preferred_element_type=jnp.float32)
        sent[:, at] = (attended * own_gate).astype(jnp.bfloat16)

    def carry():
        return pltpu.make_async_remote_copy(
            src_ref=sent,
            dst_ref=carried,
            send_sem=carry_send_sem,
            recv_sem=carry_recv_sem,
            device_id={"frame": lax.rem(me + n - 1, n)},
            device_id_type=MESH,
        )

    @pl.when(me > 0)
    def _():
        carry().start()

    column = lax.broadcasted_iota(jnp.int32, (ROWS, total), 1)
    token = lax.broadcasted_iota(jnp.int32, (ROWS, total), 0)
    same = lax.rem(column, ROWS) == token
    column_frame = lax.div(column, ROWS)

    def stamp(g, stamps):
        return jnp.where(column_frame == g, times_ref[g].astype(jnp.float32), stamps)

    stamps = lax.fori_loop(0, n, stamp, jnp.zeros((ROWS, total), jnp.float32))

    @pl.loop(0, n)
    def _(f):
        gap = jnp.abs(times_ref[f].astype(jnp.float32) - stamps)
        dist[pl.ds(pl.multiple_of(f * ROWS, ROWS), ROWS), :] = jnp.where(same, gap, FAR)

    group = math.gcd(n, 16)

    def temporal_block(chunk, head, start):
        at = pl.ds(head * head_dim, head_dim)
        rows = pl.ds(start * ROWS, group * ROWS) if isinstance(start, int) else pl.ds(
            pl.multiple_of(start * ROWS, ROWS), group * ROWS
        )
        slope = slopes_ref[first_head + chunk * (cols // head_dim) + head]
        raw = scores_of(recv[chunk, 0, rows, at], recv[chunk, 1, :, at])
        weights = softmax_rows(raw * scale - slope * dist[rows, :])
        attended = jnp.dot(weights, recv[chunk, 2, :, at], preferred_element_type=jnp.float32)
        gates = noise_gate[pl.ds(start, group), :]
        gated = attended.reshape(group, ROWS, head_dim) * gates[:, None, :]
        temporal[chunk, rows, at] = gated.reshape(group * ROWS, head_dim).astype(jnp.bfloat16)

    for chunk in range(chunks):
        whole = recv.at[chunk]
        pltpu.make_async_copy(whole, whole, recv_sem.at[chunk]).wait()
        for head in range(cols // head_dim):
            if n == group:
                temporal_block(chunk, head, 0)
            else:
                @pl.loop(0, n // group)
                def _(i):
                    temporal_block(chunk, head, i * group)

        @pl.loop(0, n)
        def _(step):
            peer = lax.rem(me + step, n)

            @pl.when(peer < n - 1)
            def _():
                source = temporal.at[chunk, pl.ds(pl.multiple_of((peer + 1) * ROWS, ROWS), ROWS), :]
                target = ret.at[chunk, my_rows, my_col]

                @pl.when(step > 0)
                def _():
                    pltpu.make_async_remote_copy(
                        src_ref=source,
                        dst_ref=target,
                        send_sem=back_send_sem.at[chunk],
                        recv_sem=back_recv_sem.at[chunk],
                        device_id={"frame": peer},
                        device_id_type=MESH,
                    ).start()

                @pl.when(step == 0)
                def _():
                    pltpu.make_async_copy(source, target, back_recv_sem.at[chunk]).start()

    @pl.when(me < n - 1)
    def _():
        carry().wait_recv()
        for chunk in range(chunks):
            whole = ret.at[chunk]
            pltpu.make_async_copy(whole, whole, back_recv_sem.at[chunk]).wait()
            for block in range(col_blocks):
                at = pl.ds(block * block_cols + chunk * cols, cols)
                out_ref[:, at] = (
                    carried[:, at].astype(jnp.float32)
                    + ret[chunk, :, block * cols:(block + 1) * cols].astype(jnp.float32)
                ).astype(jnp.bfloat16)

    @pl.when(me == n - 1)
    def _():
        out_ref[...] = jnp.zeros_like(out_ref)

    @pl.when(me > 0)
    def _():
        carry().wait_send()

    for chunk in range(chunks):
        part = recv.at[chunk, :, pl.ds(0, total - ROWS), :]
        pltpu.make_async_copy(part, part, send_sem.at[chunk]).wait()

        @pl.when(me < n - 1)
        def _():
            part = temporal.at[chunk, pl.ds(0, total - 2 * ROWS), :]
            pltpu.make_async_copy(part, part, back_send_sem.at[chunk]).wait()

        @pl.when(me == n - 1)
        def _():
            part = temporal.at[chunk, pl.ds(0, total - ROWS), :]
            pltpu.make_async_copy(part, part, back_send_sem.at[chunk]).wait()


def body(queries, key_rows, value_rows, slopes, noise_level, frame_times):
    n = lax.axis_size("frame")
    frame_rows, width = queries.shape
    head_count = slopes.shape[0]
    head_dim = width // head_count
    row_blocks = frame_rows // ROWS
    col_blocks = n // row_blocks
    block_cols = width // col_blocks
    chunks = math.gcd(block_cols // head_dim, 4)
    cols = block_cols // chunks
    total = n * ROWS
    plan = (frame_rows, width, head_count, head_dim, row_blocks, col_blocks, chunks)
    bf16, f32 = jnp.bfloat16, jnp.float32
    smem = pl.BlockSpec(memory_space=pltpu.SMEM)
    anywhere = pl.BlockSpec(memory_space=pl.ANY)
    return pl.pallas_call(
        functools.partial(kernel, n, plan),
        out_shape=jax.ShapeDtypeStruct((frame_rows, width), bf16),
        in_specs=[smem] * 3 + [anywhere] * 3,
        out_specs=pl.BlockSpec(memory_space=pltpu.VMEM),
        scratch_shapes=[
            pltpu.VMEM((3, frame_rows, width), bf16),
            pltpu.VMEM((chunks, 3, total, cols), bf16),
            pltpu.VMEM((chunks, total, cols), bf16),
            pltpu.VMEM((chunks, frame_rows, col_blocks * cols), bf16),
            pltpu.VMEM((frame_rows, width), bf16),
            pltpu.VMEM((frame_rows, width), bf16),
            pltpu.VMEM((total, total), f32),
            pltpu.VMEM((n, LANES), f32),
            pltpu.VMEM((n, LANES), f32),
            pltpu.SemaphoreType.DMA((3,)),
            pltpu.SemaphoreType.DMA((chunks,)),
            pltpu.SemaphoreType.DMA((chunks,)),
            pltpu.SemaphoreType.DMA((chunks,)),
            pltpu.SemaphoreType.DMA((chunks,)),
            pltpu.SemaphoreType.DMA,
            pltpu.SemaphoreType.DMA,
        ],
        compiler_params=pltpu.CompilerParams(
            collective_id=0, has_side_effects=True, vmem_limit_bytes=48 * 1024 * 1024
        ),
    )(slopes.astype(f32), noise_level, frame_times, queries, key_rows, value_rows)


def solution(mesh):
    return jax.shard_map(
        body,
        mesh=mesh,
        in_specs=(
            P(("groups", "frame"), None),
            P(("groups", "frame"), None),
            P(("groups", "frame"), None),
            P(),
            P("groups"),
            P("groups"),
        ),
        out_specs=P(("groups", "frame"), None),
        check_vma=False,
    )
```

time: 88.7 us -> 63.6 us (0.72)
  the two profiles are of different devices: /device:TPU:13 before, /device:TPU:0 now
where the time goes in v1:
time: 63.6 us; the launch traced here: 63.3 us
  Pallas kernels  58.7 us (92%)
  local copies, waits for them, and re-layouts  3.93 us (6%)
  other arithmetic  0.68 us (1%)
    pallas_call x1, Pallas kernels, body(): pl.pallas_call(functools.partial(kernel, n, plan), out_shape=jax.ShapeDty...  58.7 us
    unnamed x11, local copies, waits for them, and re-layouts  3.93 us

profile of v1, /device:TPU:0, one launch (start us, length us, event | category | flops | bytes accessed | tf_op | source)
XLA Modules:
  0.0 63.3 jit_solution(3753930619099856617)
XLA Ops:
  0.0 0.0 copy-start.4
  0.0 0.0 copy-start.3
  0.0 0.7 %convert_element_type.3.slopes_ref = f32[16]{0:T(128)S(1)} convert(bf16[16]{0:T(256)(128)(2,1)} %param.9) | non-fusion elementwise | flops 16 | bytes 96 | tf_op jit(solution)/shard_map/convert_element_type | solution.py:266
  0.7 0.0 copy-done.4
  0.7 0.0 copy-done.3
  0.7 0.0 copy-start
  0.7 1.0 %copy-done = bf16[128,2048]{1,0:T(8,128)(2,1)S(1)} copy-done((bf16[128,2048]{1,0:T(8,128)(2,1)S(1)}, bf16[128,2048]{1,0:T(8,128)(2,1)}, u32[]{:S(2)}) %copy-start) | copy-done | bytes 524312
  1.7 0.0 copy-start.1
  1.7 1.0 %copy-done.1 = bf16[128,2048]{1,0:T(8,128)(2,1)S(1)} copy-done((bf16[128,2048]{1,0:T(8,128)(2,1)S(1)}, bf16[128,2048]{1,0:T(8,128)(2,1)}, u32[]{:S(2)}) %copy-start.1) | copy-done | bytes 524312
  2.8 0.0 copy-start.2
  2.8 1.0 %copy-done.2 = bf16[128,2048]{1,0:T(8,128)(2,1)S(1)} copy-done((bf16[128,2048]{1,0:T(8,128)(2,1)S(1)}, bf16[128,2048]{1,0:T(8,128)(2,1)}, u32[]{:S(2)}) %copy-start.2) | copy-done | bytes 524312
  3.8 58.7 %shard_map.64 = bf16[128,2048]{1,0:T(8,128)(2,1)S(1)} custom-call(f32[16]{0:T(128)S(1)} %convert_element_type.3.slopes_ref, s32[16]{0:T(128)S(1)} %copy-done.3, s32[16]{0:T(128)S(1)} %copy-done.4, bf16[128,2048]{1,0:T(8,128)(2,1)S(1)} %copy-done, bf16[128,2048]{1,0:T(8,128)(2,1)S(1)} %copy-done.1, bf16[128,2048]{1,0:T(8,128)(2,1)S(1)} %copy-done.2), custom_call_target="tpu_custom_call" | custom-call | tf_op jit(solution)/shard_map/pallas_call | solution.py:240
  62.5 0.8 %copy.8 = bf16[128,2048]{1,0:T(8,128)(2,1)} copy(bf16[128,2048]{1,0:T(8,128)(2,1)S(1)} %shard_map.64) | data formatting | bytes 1048576
Async XLA Ops:
  0.0 0.7 %copy-start.4 = (s32[16]{0:T(128)S(1)}, s32[16]{0:T(128)}, u32[]{:S(2)}) copy-start(s32[16]{0:T(128)} %times_ref.1) | copy-start | bytes 196
  0.0 0.7 %copy-start.3 = (s32[16]{0:T(128)S(1)}, s32[16]{0:T(128)}, u32[]{:S(2)}) copy-start(s32[16]{0:T(128)} %level_ref.1) | copy-start | bytes 196
  0.7 1.0 %copy-start = (bf16[128,2048]{1,0:T(8,128)(2,1)S(1)}, bf16[128,2048]{1,0:T(8,128)(2,1)}, u32[]{:S(2)}) copy-start(bf16[128,2048]{1,0:T(8,128)(2,1)} %q_ref.1) | copy-start | bytes 1572868
  1.7 1.0 %copy-start.1 = (bf16[128,2048]{1,0:T(8,128)(2,1)S(1)}, bf16[128,2048]{1,0:T(8,128)(2,1)}, u32[]{:S(2)}) copy-start(bf16[128,2048]{1,0:T(8,128)(2,1)} %k_ref.1) | copy-start | bytes 1572868
  2.8 1.0 %copy-start.2 = (bf16[128,2048]{1,0:T(8,128)(2,1)S(1)}, bf16[128,2048]{1,0:T(8,128)(2,1)}, u32[]{:S(2)}) copy-start(bf16[128,2048]{1,0:T(8,128)(2,1)} %v_ref.1) | copy-start | bytes 1572868

commit v2 on v1

--- a/solution.py
+++ b/solution.py
@@ -29,23 +29,30 @@
 
 def kernel(
     n, plan,
-    slopes_ref, level_ref, times_ref, q_ref, k_ref, v_ref, out_ref,
-    qkv, recv, temporal, ret, sent, carried, dist, signal_gate, noise_gate,
+    slopes_hbm, level_hbm, times_hbm, q_ref, k_ref, v_ref, out_ref,
+    qkv, recv, temporal, ret, sent, carried, middle, mixed, dist, signal_gate, noise_gate,
+    slopes_ref, level_ref, times_ref, slope_rows,
     load_sem, send_sem, recv_sem, back_send_sem, back_recv_sem, carry_send_sem, carry_recv_sem,
+    middle_send_sem, middle_recv_sem, mixed_send_sem,
 ):
     frame_rows, width, head_count, head_dim, row_blocks, col_blocks, chunks = plan
     block_cols = width // col_blocks
     cols = block_cols // chunks
     total = n * ROWS
     scale = 1.0 / math.sqrt(head_dim)
+    half = n // 2
     me = lax.axis_index("frame")
 
     loads = [
         pltpu.make_async_copy(source, qkv.at[i], load_sem.at[i])
         for i, source in enumerate((q_ref, k_ref, v_ref))
     ]
-    for load in loads:
-        load.start()
+    small = [
+        pltpu.make_async_copy(source, target, load_sem.at[3 + i])
+        for i, (source, target) in enumerate(
+            ((slopes_hbm, slopes_ref), (level_hbm, level_ref), (times_hbm, times_ref))
+        )
+    ]
     barrier = pltpu.get_barrier_semaphore()
 
     @pl.loop(1, n)
@@ -54,9 +61,16 @@
             barrier, inc=1, device_id={"frame": lax.rem(me + step, n)}, device_id_type=MESH
         )
 
+    for load in loads + small:
+        load.start()
     pl.semaphore_wait(barrier, n - 1)
     for load in loads:
         load.wait()
+
+    def block_at(peer):
+        row = pl.multiple_of(lax.div(peer, col_blocks) * ROWS, ROWS)
+        col = pl.multiple_of(lax.rem(peer, col_blocks) * block_cols, LANES)
+        return pl.ds(row, ROWS), pl.ds(col, block_cols)
 
     def piece(peer, chunk):
         row = pl.multiple_of(lax.div(peer, col_blocks) * ROWS, ROWS)
@@ -86,6 +100,15 @@
             piece(me, chunk), recv.at[chunk, :, my_slot, :], recv_sem.at[chunk]
         ).start()
 
+    for load in small:
+        load.wait()
+    square = (head_count, head_count)
+    diagonal = lax.broadcasted_iota(jnp.int32, square, 0) == lax.broadcasted_iota(jnp.int32, square, 1)
+    spread = jnp.broadcast_to(slopes_ref[...].astype(jnp.float32).reshape(1, head_count), square)
+    slope_rows[...] = jnp.broadcast_to(
+        jnp.sum(jnp.where(diagonal, spread, 0.0), axis=1, keepdims=True), slope_rows.shape
+    )
+
     row_frame = lax.broadcasted_iota(jnp.int32, (n, LANES), 0)
 
     def place(f, level):
@@ -117,9 +140,27 @@
             device_id_type=MESH,
         )
 
-    @pl.when(me > 0)
+    carries = (me > 0) & (me != half)
+
+    @pl.when(carries)
     def _():
         carry().start()
+
+    @pl.when(me == half)
+    def _():
+        @pl.loop(1, n)
+        def _(step):
+            peer = lax.rem(me + step, n)
+            pltpu.make_async_remote_copy(
+                src_ref=sent.at[block_at(peer)],
+                dst_ref=middle,
+                send_sem=middle_send_sem,
+                recv_sem=middle_recv_sem,
+                device_id={"frame": peer},
+                device_id_type=MESH,
+            ).start()
+
+        pltpu.make_async_copy(sent.at[block_at(me)], middle, middle_recv_sem).start()
 
     column = lax.broadcasted_iota(jnp.int32, (ROWS, total), 1)
     token = lax.broadcasted_iota(jnp.int32, (ROWS, total), 0)
@@ -143,7 +184,7 @@
         rows = pl.ds(start * ROWS, group * ROWS) if isinstance(start, int) else pl.ds(
             pl.multiple_of(start * ROWS, ROWS), group * ROWS
         )
-        slope = slopes_ref[first_head + chunk * (cols // head_dim) + head]
+        slope = slope_rows[pl.ds(first_head + chunk * (cols // head_dim) + head, 1), :][:, :1]
         raw = scores_of(recv[chunk, 0, rows, at], recv[chunk, 1, :, at])
         weights = softmax_rows(raw * scale - slope * dist[rows, :])
         attended = jnp.dot(weights, recv[chunk, 2, :, at], preferred_element_type=jnp.float32)
@@ -166,7 +207,7 @@
         def _(step):
             peer = lax.rem(me + step, n)
 
-            @pl.when(peer < n - 1)
+            @pl.when((peer < n - 1) & (peer != half - 1))
             def _():
                 source = temporal.at[chunk, pl.ds(pl.multiple_of((peer + 1) * ROWS, ROWS), ROWS), :]
                 target = ret.at[chunk, my_rows, my_col]
@@ -186,9 +227,35 @@
                 def _():
                     pltpu.make_async_copy(source, target, back_recv_sem.at[chunk]).start()
 
-    @pl.when(me < n - 1)
-    def _():
-        carry().wait_recv()
+    pltpu.make_async_copy(middle, middle, middle_recv_sem).wait()
+    for chunk in range(chunks):
+        at = pl.ds(chunk * cols, cols)
+        mixed[:, at] = (
+            temporal[chunk, half * ROWS:(half + 1) * ROWS, :].astype(jnp.float32)
+            + middle[:, at].astype(jnp.float32)
+        ).astype(jnp.bfloat16)
+    last = pltpu.make_async_remote_copy(
+        src_ref=mixed,
+        dst_ref=carried.at[block_at(me)],
+        send_sem=mixed_send_sem,
+        recv_sem=carry_recv_sem,
+        device_id={"frame": half - 1},
+        device_id_type=MESH,
+    )
+
+    @pl.when(me != half - 1)
+    def _():
+        last.start()
+
+    @pl.when(me == half - 1)
+    def _():
+        pltpu.make_async_copy(mixed, carried.at[block_at(me)], carry_recv_sem).start()
+        pltpu.make_async_copy(carried, carried, carry_recv_sem).wait()
+        out_ref[...] = carried[...]
+
+    @pl.when((me < n - 1) & (me != half - 1))
+    def _():
+        pltpu.make_async_copy(carried, carried, carry_recv_sem).wait()
         for chunk in range(chunks):
             whole = ret.at[chunk]
             pltpu.make_async_copy(whole, whole, back_recv_sem.at[chunk]).wait()
@@ -203,22 +270,33 @@
     def _():
         out_ref[...] = jnp.zeros_like(out_ref)
 
-    @pl.when(me > 0)
+    @pl.when(carries)
     def _():
         carry().wait_send()
+
+    @pl.when(me == half)
+    def _():
+        part = temporal.at[:, pl.ds(0, total - ROWS), :]
+        pltpu.make_async_copy(part, part, middle_send_sem).wait()
+
+    @pl.when(me != half - 1)
+    def _():
+        last.wait_send()
+
+    ends = (me == n - 1) | (me == half - 1)
 
     for chunk in range(chunks):
         part = recv.at[chunk, :, pl.ds(0, total - ROWS), :]
         pltpu.make_async_copy(part, part, send_sem.at[chunk]).wait()
 
-        @pl.when(me < n - 1)
+        @pl.when(jnp.logical_not(ends))
+        def _():
+            part = temporal.at[chunk, pl.ds(0, total - 3 * ROWS), :]
+            pltpu.make_async_copy(part, part, back_send_sem.at[chunk]).wait()
+
+        @pl.when(ends)
         def _():
             part = temporal.at[chunk, pl.ds(0, total - 2 * ROWS), :]
-            pltpu.make_async_copy(part, part, back_send_sem.at[chunk]).wait()
-
-        @pl.when(me == n - 1)
-        def _():
-            part = temporal.at[chunk, pl.ds(0, total - ROWS), :]
             pltpu.make_async_copy(part, part, back_send_sem.at[chunk]).wait()
 
 
@@ -235,12 +313,11 @@
     total = n * ROWS
     plan = (frame_rows, width, head_count, head_dim, row_blocks, col_blocks, chunks)
     bf16, f32 = jnp.bfloat16, jnp.float32
-    smem = pl.BlockSpec(memory_space=pltpu.SMEM)
-    anywhere = pl.BlockSpec(memory_space=pl.ANY)
+    anywhere = pl.BlockSpec(memory_space=pltpu.HBM)
     return pl.pallas_call(
         functools.partial(kernel, n, plan),
         out_shape=jax.ShapeDtypeStruct((frame_rows, width), bf16),
-        in_specs=[smem] * 3 + [anywhere] * 3,
+        in_specs=[anywhere] * 6,
         out_specs=pl.BlockSpec(memory_space=pltpu.VMEM),
         scratch_shapes=[
             pltpu.VMEM((3, frame_rows, width), bf16),
@@ -249,21 +326,30 @@
             pltpu.VMEM((chunks, frame_rows, col_blocks * cols), bf16),
             pltpu.VMEM((frame_rows, width), bf16),
             pltpu.VMEM((frame_rows, width), bf16),
+            pltpu.VMEM((ROWS, block_cols), bf16),
+            pltpu.VMEM((ROWS, block_cols), bf16),
             pltpu.VMEM((total, total), f32),
             pltpu.VMEM((n, LANES), f32),
             pltpu.VMEM((n, LANES), f32),
-            pltpu.SemaphoreType.DMA((3,)),
+            pltpu.VMEM(slopes.shape, slopes.dtype),
+            pltpu.SMEM(noise_level.shape, noise_level.dtype),
+            pltpu.SMEM(frame_times.shape, frame_times.dtype),
+            pltpu.VMEM((head_count, LANES), f32),
+            pltpu.SemaphoreType.DMA((6,)),
             pltpu.SemaphoreType.DMA((chunks,)),
             pltpu.SemaphoreType.DMA((chunks,)),
             pltpu.SemaphoreType.DMA((chunks,)),
             pltpu.SemaphoreType.DMA((chunks,)),
             pltpu.SemaphoreType.DMA,
             pltpu.SemaphoreType.DMA,
+            pltpu.SemaphoreType.DMA,
+            pltpu.SemaphoreType.DMA,
+            pltpu.SemaphoreType.DMA,
         ],
         compiler_params=pltpu.CompilerParams(
-            collective_id=0, has_side_effects=True, vmem_limit_bytes=48 * 1024 * 1024
+            collective_id=0, has_side_effects=True, vmem_limit_bytes=64 * 1024 * 1024
         ),
-    )(slopes.astype(f32), noise_level, frame_times, queries, key_rows, value_rows)
+    )(slopes, noise_level, frame_times, queries, key_rows, value_rows)
 
 
 def solution(mesh):

time: 63.6 us -> 57.7 us (0.907)
  Pallas kernels: 58.7 us -> 55.7 us
  local copies, waits for them, and re-layouts: 3.93 us -> 1.88 us
  other arithmetic: 0.68 us -> 0 us
    pallas_call x1, Pallas kernels: 58.7 us -> 55.7 us  [body(): pl.pallas_call(functools.partial(kernel, n, plan), out_shape=jax.ShapeDty...]
    unnamed x11 -> x1, local copies, waits for them, and re-layouts: 3.93 us -> 1.88 us
    convert_element_type x1 -> x0, other arithmetic: 0.68 us -> none  [body(): slopes.astype(f32)]
where the time goes in v2:
time: 57.7 us; the launch traced here: 57.6 us
  Pallas kernels  55.7 us (97%)
  local copies, waits for them, and re-layouts  1.88 us (3%)
    pallas_call x1, Pallas kernels, body(): pl.pallas_call(functools.partial(kernel, n, plan), out_shape=jax.ShapeDty...  55.7 us
    unnamed x1, local copies, waits for them, and re-layouts  1.88 us

profile of v2, /device:TPU:0, one launch (start us, length us, event | category | flops | bytes accessed | tf_op | source)
XLA Modules:
  0.0 57.6 jit_solution(10446030888387845722)
XLA Ops:
  0.0 55.7 %shard_map.64 = bf16[128,2048]{1,0:T(8,128)(2,1)} custom-call(bf16[16]{0:T(256)(128)(2,1)} %slopes_hbm.1, s32[16]{0:T(128)} %level_hbm.1, s32[16]{0:T(128)} %times_hbm.1, bf16[128,2048]{1,0:T(8,128)(2,1)} %q_ref.1, bf16[128,2048]{1,0:T(8,128)(2,1)} %k_ref.1, bf16[128,2048]{1,0:T(8,128)(2,1)} %v_ref.1), custom_call_target="tpu_custom_call" | custom-call | tf_op jit(solution)/shard_map/pallas_call | solution.py:317
  55.7 1.9 %copy.8 = bf16[128,2048]{1,0:T(8,128)(2,1)} copy(bf16[128,2048]{1,0:T(8,128)(2,1)} %shard_map.64) | data formatting | bytes 1048576

commit v3 on v2

--- a/solution.py
+++ b/solution.py
@@ -33,7 +33,7 @@
     qkv, recv, temporal, ret, sent, carried, middle, mixed, dist, signal_gate, noise_gate,
     slopes_ref, level_ref, times_ref, slope_rows,
     load_sem, send_sem, recv_sem, back_send_sem, back_recv_sem, carry_send_sem, carry_recv_sem,
-    middle_send_sem, middle_recv_sem, mixed_send_sem,
+    middle_send_sem, middle_recv_sem, mixed_send_sem, second, third, fourth,
 ):
     frame_rows, width, head_count, head_dim, row_blocks, col_blocks, chunks = plan
     block_cols = width // col_blocks
@@ -55,15 +55,42 @@
     ]
     barrier = pltpu.get_barrier_semaphore()
 
-    @pl.loop(1, n)
-    def _(step):
+    part_size = n // 4
+    quarter, place_in = lax.div(me, part_size), lax.rem(me, part_size)
+    inner = (quarter == 1) | (quarter == 2)
+    across = 3 - quarter
+    outer = jnp.where(quarter == 1, 0, 3)
+    beside = jnp.where(quarter == 0, 1, 2)
+
+    def tell(semaphore, where, slot):
         pl.semaphore_signal(
-            barrier, inc=1, device_id={"frame": lax.rem(me + step, n)}, device_id_type=MESH
+            semaphore, inc=1, device_id={"frame": where * part_size + slot}, device_id_type=MESH
         )
+
+    @pl.when(inner)
+    def _():
+        @pl.loop(0, part_size)
+        def _(slot):
+            tell(barrier, across, slot)
+
+        @pl.loop(0, part_size)
+        def _(slot):
+            tell(barrier, outer, slot)
 
     for load in loads + small:
         load.start()
-    pl.semaphore_wait(barrier, n - 1)
+    pl.semaphore_wait(barrier, part_size)
+
+    @pl.when(inner)
+    def _():
+        tell(second, across, place_in)
+
+    @pl.when(jnp.logical_not(inner))
+    def _():
+        @pl.loop(0, part_size)
+        def _(slot):
+            tell(second, beside, slot)
+
     for load in loads:
         load.wait()
 
@@ -81,20 +108,45 @@
     my_rows = pl.ds(pl.multiple_of(lax.div(me, col_blocks) * ROWS, ROWS), ROWS)
     my_col = pl.ds(pl.multiple_of(lax.rem(me, col_blocks) * cols, LANES), cols)
     first_head = lax.rem(me, col_blocks) * (block_cols // head_dim)
+
+    def send(peer, chunk):
+        pltpu.make_async_remote_copy(
+            src_ref=piece(peer, chunk),
+            dst_ref=recv.at[chunk, :, my_slot, :],
+            send_sem=send_sem.at[chunk],
+            recv_sem=recv_sem.at[chunk],
+            device_id={"frame": peer},
+            device_id_type=MESH,
+        ).start()
+
+    @pl.when(inner)
+    def _():
+        @pl.loop(0, chunks)
+        def _(chunk):
+            @pl.loop(0, part_size)
+            def _(step):
+                send(across * part_size + lax.rem(place_in + step, part_size), chunk)
+
+        pl.semaphore_wait(second, part_size + 1)
+        tell(third, outer, place_in)
+        tell(third, across, place_in)
+        pl.semaphore_wait(third, 1)
+        tell(fourth, outer, place_in)
+
+    @pl.when(jnp.logical_not(inner))
+    def _():
+        pl.semaphore_wait(third, 1)
+        pl.semaphore_wait(fourth, 1)
 
     @pl.loop(0, chunks)
     def _(chunk):
         @pl.loop(1, n)
         def _(step):
             peer = lax.rem(me + step, n)
-            pltpu.make_async_remote_copy(
-                src_ref=piece(peer, chunk),
-                dst_ref=recv.at[chunk, :, my_slot, :],
-                send_sem=send_sem.at[chunk],
-                recv_sem=recv_sem.at[chunk],
-                device_id={"frame": peer},
-                device_id_type=MESH,
-            ).start()
+
+            @pl.when(jnp.logical_not(inner & (lax.div(peer, part_size) == across)))
+            def _():
+                send(peer, chunk)
 
         pltpu.make_async_copy(
             piece(me, chunk), recv.at[chunk, :, my_slot, :], recv_sem.at[chunk]
@@ -308,7 +360,7 @@
     row_blocks = frame_rows // ROWS
     col_blocks = n // row_blocks
     block_cols = width // col_blocks
-    chunks = math.gcd(block_cols // head_dim, 4)
+    chunks = math.gcd(block_cols // head_dim, 2)
     cols = block_cols // chunks
     total = n * ROWS
     plan = (frame_rows, width, head_count, head_dim, row_blocks, col_blocks, chunks)
@@ -345,6 +397,9 @@
             pltpu.SemaphoreType.DMA,
             pltpu.SemaphoreType.DMA,
             pltpu.SemaphoreType.DMA,
+            pltpu.SemaphoreType.REGULAR,
+            pltpu.SemaphoreType.REGULAR,
+            pltpu.SemaphoreType.REGULAR,
         ],
         compiler_params=pltpu.CompilerParams(
             collective_id=0, has_side_effects=True, vmem_limit_bytes=64 * 1024 * 1024

time: 57.7 us -> 55.9 us (0.969)
  Pallas kernels: 55.7 us -> 53.9 us
    pallas_call x1, Pallas kernels: 55.7 us -> 53.9 us  [body(): pl.pallas_call(functools.partial(kernel, n, plan), out_shape=jax.ShapeDty...]
where the time goes in v3:
time: 55.9 us; the launch traced here: 55.8 us
  Pallas kernels  53.9 us (96%)
  local copies, waits for them, and re-layouts  1.88 us (3%)
    pallas_call x1, Pallas kernels, body(): pl.pallas_call(functools.partial(kernel, n, plan), out_shape=jax.ShapeDty...  53.9 us
    unnamed x1, local copies, waits for them, and re-layouts  1.88 us

profile of v3, /device:TPU:0, one launch (start us, length us, event | category | flops | bytes accessed | tf_op | source)
XLA Modules:
  0.0 55.8 jit_solution(11812355070789850548)
XLA Ops:
  0.0 53.9 %shard_map.64 = bf16[128,2048]{1,0:T(8,128)(2,1)} custom-call(bf16[16]{0:T(256)(128)(2,1)} %slopes_hbm.1, s32[16]{0:T(128)} %level_hbm.1, s32[16]{0:T(128)} %times_hbm.1, bf16[128,2048]{1,0:T(8,128)(2,1)} %q_ref.1, bf16[128,2048]{1,0:T(8,128)(2,1)} %k_ref.1, bf16[128,2048]{1,0:T(8,128)(2,1)} %v_ref.1), custom_call_target="tpu_custom_call" | custom-call | tf_op jit(solution)/shard_map/pallas_call | solution.py:369
  53.9 1.9 %copy.8 = bf16[128,2048]{1,0:T(8,128)(2,1)} copy(bf16[128,2048]{1,0:T(8,128)(2,1)} %shard_map.64) | data formatting | bytes 1048576

commit v4 on v3

--- a/solution.py
+++ b/solution.py
@@ -34,6 +34,7 @@
     slopes_ref, level_ref, times_ref, slope_rows,
     load_sem, send_sem, recv_sem, back_send_sem, back_recv_sem, carry_send_sem, carry_recv_sem,
     middle_send_sem, middle_recv_sem, mixed_send_sem, second, third, fourth,
+    relay, relay_send_sem, relay_recv_sem, relay_out_sem,
 ):
     frame_rows, width, head_count, head_dim, row_blocks, col_blocks, chunks = plan
     block_cols = width // col_blocks
@@ -193,6 +194,15 @@
         )
 
     carries = (me > 0) & (me != half)
+    relay_device = half + part_size // 2
+    handed = pltpu.make_async_remote_copy(
+        src_ref=sent.at[pl.ds(frame_rows // 4, frame_rows // 4), :],
+        dst_ref=relay,
+        send_sem=relay_send_sem,
+        recv_sem=relay_recv_sem,
+        device_id={"frame": relay_device},
+        device_id_type=MESH,
+    )
 
     @pl.when(carries)
     def _():
@@ -203,16 +213,20 @@
         @pl.loop(1, n)
         def _(step):
             peer = lax.rem(me + step, n)
-            pltpu.make_async_remote_copy(
-                src_ref=sent.at[block_at(peer)],
-                dst_ref=middle,
-                send_sem=middle_send_sem,
-                recv_sem=middle_recv_sem,
-                device_id={"frame": peer},
-                device_id_type=MESH,
-            ).start()
+
+            @pl.when((peer < half // 2) | (peer >= half))
+            def _():
+                pltpu.make_async_remote_copy(
+                    src_ref=sent.at[block_at(peer)],
+                    dst_ref=middle,
+                    send_sem=middle_send_sem,
+                    recv_sem=middle_recv_sem,
+                    device_id={"frame": peer},
+                    device_id_type=MESH,
+                ).start()
 
         pltpu.make_async_copy(sent.at[block_at(me)], middle, middle_recv_sem).start()
+        handed.start()
 
     column = lax.broadcasted_iota(jnp.int32, (ROWS, total), 1)
     token = lax.broadcasted_iota(jnp.int32, (ROWS, total), 0)
@@ -245,6 +259,25 @@
         temporal[chunk, rows, at] = gated.reshape(group * ROWS, head_dim).astype(jnp.bfloat16)
 
     for chunk in range(chunks):
+        if chunk == chunks - 1:
+            @pl.when(me == relay_device)
+            def _():
+                handed.wait_recv()
+
+                @pl.loop(half // 2, half)
+                def _(peer):
+                    row = pl.multiple_of(
+                        lax.div(peer, col_blocks) * ROWS - frame_rows // 4, ROWS
+                    )
+                    pltpu.make_async_remote_copy(
+                        src_ref=relay.at[pl.ds(row, ROWS), block_at(peer)[1]],
+                        dst_ref=middle,
+                        send_sem=relay_out_sem,
+                        recv_sem=middle_recv_sem,
+                        device_id={"frame": peer},
+                        device_id_type=MESH,
+                    ).start()
+
         whole = recv.at[chunk]
         pltpu.make_async_copy(whole, whole, recv_sem.at[chunk]).wait()
         for head in range(cols // head_dim):
@@ -328,8 +361,14 @@
 
     @pl.when(me == half)
     def _():
-        part = temporal.at[:, pl.ds(0, total - ROWS), :]
+        part = temporal.at[:, pl.ds(0, total - (1 + half // 2) * ROWS), :]
         pltpu.make_async_copy(part, part, middle_send_sem).wait()
+        handed.wait_send()
+
+    @pl.when(me == relay_device)
+    def _():
+        part = temporal.at[:, pl.ds(0, half // 2 * ROWS), :]
+        pltpu.make_async_copy(part, part, relay_out_sem).wait()
 
     @pl.when(me != half - 1)
     def _():
@@ -400,6 +439,10 @@
             pltpu.SemaphoreType.REGULAR,
             pltpu.SemaphoreType.REGULAR,
             pltpu.SemaphoreType.REGULAR,
+            pltpu.VMEM((frame_rows // 4, width), bf16),
+            pltpu.SemaphoreType.DMA,
+            pltpu.SemaphoreType.DMA,
+            pltpu.SemaphoreType.DMA,
         ],
         compiler_params=pltpu.CompilerParams(
             collective_id=0, has_side_effects=True, vmem_limit_bytes=64 * 1024 * 1024

time: 55.9 us -> 54.6 us (0.977)
  Pallas kernels: 53.9 us -> 52.5 us
    pallas_call x1, Pallas kernels: 53.9 us -> 52.5 us  [body(): pl.pallas_call(functools.partial(kernel, n, plan), out_shape=jax.ShapeDty...]
where the time goes in v4:
time: 54.6 us; the launch traced here: 54.4 us
  Pallas kernels  52.5 us (96%)
  local copies, waits for them, and re-layouts  1.88 us (3%)
    pallas_call x1, Pallas kernels, body(): pl.pallas_call(functools.partial(kernel, n, plan), out_shape=jax.ShapeDty...  52.5 us
    unnamed x1, local copies, waits for them, and re-layouts  1.88 us

profile of v4, /device:TPU:0, one launch (start us, length us, event | category | flops | bytes accessed | tf_op | source)
XLA Modules:
  0.0 54.4 jit_solution(14764099895293418005)
XLA Ops:
  0.0 52.5 %shard_map.64 = bf16[128,2048]{1,0:T(8,128)(2,1)} custom-call(bf16[16]{0:T(256)(128)(2,1)} %slopes_hbm.1, s32[16]{0:T(128)} %level_hbm.1, s32[16]{0:T(128)} %times_hbm.1, bf16[128,2048]{1,0:T(8,128)(2,1)} %q_ref.1, bf16[128,2048]{1,0:T(8,128)(2,1)} %k_ref.1, bf16[128,2048]{1,0:T(8,128)(2,1)} %v_ref.1), custom_call_target="tpu_custom_call" | custom-call | tf_op jit(solution)/shard_map/pallas_call | solution.py:408
  52.5 1.9 %copy.8 = bf16[128,2048]{1,0:T(8,128)(2,1)} copy(bf16[128,2048]{1,0:T(8,128)(2,1)} %shard_map.64) | data formatting | bytes 1048576
